TPU v7x, 32 devices: a whole 2x2x4 slice. The times are simulated.
32 devices in a mesh: dp: 4 (over z), group: 4 (over x, core), tensor: 2 (over y).
Axes of the slice: x: 2, y: 2, z: 4, core: 2. Of those that a mesh axis runs over, the one named last changes fastest.
Arguments:
- attn_heads: bfloat16 [256, 8192], P('dp', ('group', 'tensor')), parts along dimension 0, may hold values from -6 to 6
- out_proj: bfloat16 [8192, 3584], P(('group', 'tensor')), may hold values from -0.0625 to 0.0625
- residual_in: bfloat16 [256, 3584], P(('dp', 'group', 'tensor')), parts along dimension 0, may hold values from -6 to 6
- norm_gain: float32 [3584], replicated, may hold values from 0.1 to 1.9
- expert_ids: int32 [256, 4], P(('dp', 'group', 'tensor')), parts along dimension 0, may hold values from 0 to 7, as said below
- gate_weights: bfloat16 [256, 4], P(('dp', 'group', 'tensor')), parts along dimension 0, may hold values from 0.19921875 to 1.5
- w_gate: bfloat16 [8, 3584, 1024], P('group', None, 'tensor'), may hold values from -0.09375 to 0.09375
- w_up: bfloat16 [8, 3584, 1024], P('group', None, 'tensor'), may hold values from -0.09375 to 0.09375
- w_down: bfloat16 [8, 1024, 3584], P('group', 'tensor'), may hold values from -0.1875 to 0.1875
Outputs:
- layer_out: bfloat16 [256, 3584], P(('dp', 'group', 'tensor')), parts along dimension 0
There are 4 independent parts, one for each index of `dp`. A program takes and returns all parts, laid end to end along the dimension named above; an argument that names none is the same for every part. Nothing has to cross between parts.
Inputs may be any that keep to these rules, and one draw needn't show every extreme that they name: `expert_ids`: each row names 4 different experts, of at most 3 node groups (expert e belongs to node group e // 2). In each aligned block of 8 rows (the rows of one device) at most 6 rows name experts of any one node group, and in every draw some node group is named by exactly 6 rows of every block.
All inputs are finite; a program needn't handle non-finite values.
Results may differ from a plain program's by a relative error of at most 0.02.
Values may be sent and summed in bfloat16 or wider, within the bound.
A program may use at most 64 MiB of HBM per device.

v0:
```python
import jax
import jax.numpy as jnp
from jax import lax
from jax.sharding import PartitionSpec as P


def slot_tables(table, groups, members, capacity):
    node_weights = table.astype(jnp.float32).reshape(table.shape[:-1] + (groups, members))
    chosen = (jnp.sum(node_weights, axis=-1) > 0).astype(jnp.float32)
    position = jnp.cumsum(chosen, axis=-2) - 1.0
    slot_ids = jnp.arange(capacity, dtype=jnp.float32)
    slot_map = chosen[..., None] * (position[..., None] == slot_ids).astype(jnp.float32)
    return (slot_map, node_weights)


def on_device(
    attn_heads, out_proj, residual_in, norm_gain, expert_ids, gate_weights, w_gate, w_up, w_down
):
    tokens_here = residual_in.shape[0]
    features = residual_in.shape[1]
    groups = lax.axis_size("group")
    tensors = lax.axis_size("tensor")
    members = w_gate.shape[0]
    experts_all = groups * members
    capacity = 3 * tokens_here // 4
    projected = lax.psum_scatter(
        jnp.dot(attn_heads, out_proj, preferred_element_type=jnp.float32).astype(jnp.bfloat16),
        ("group", "tensor"),
        scatter_dimension=0,
        tiled=True,
    )
    hidden = (residual_in.astype(jnp.float32) + projected.astype(jnp.float32)).astype(jnp.bfloat16)
    stream = hidden.astype(jnp.float32)
    scale = lax.rsqrt(jnp.mean(stream * stream, axis=1, keepdims=True) + 1e-06)
    normed = (stream * scale * norm_gain).astype(jnp.bfloat16)
    matches = (
        expert_ids[:, :, None] == jnp.arange(experts_all, dtype=jnp.int32)[None, None, :]
    ).astype(jnp.float32)
    table = jnp.sum(matches * gate_weights.astype(jnp.float32)[:, :, None], axis=1).astype(
        jnp.bfloat16
    )
    slot_map, node_weights = slot_tables(table, groups, members, capacity)
    slot_bf = slot_map.astype(jnp.bfloat16)
    send_rows = jnp.einsum(
        "rgc,rd->gcd", slot_bf, normed, preferred_element_type=jnp.float32
    ).astype(jnp.bfloat16)
    send_weights = jnp.einsum("rgc,rgj->gcj", slot_map, node_weights).astype(jnp.bfloat16)
    arrived = (
        lax.all_to_all(send_rows, "group", split_axis=0, concat_axis=0, tiled=True),
        lax.all_to_all(send_weights, "group", split_axis=0, concat_axis=0, tiled=True),
    )
    rows_all, weights_all = (
        lax.all_gather(arrived[0][:, None], "tensor", axis=1, tiled=True),
        lax.all_gather(arrived[1][:, None], "tensor", axis=1, tiled=True),
    )
    received = rows_all.reshape(-1, features)
    expert_weights = weights_all.reshape(-1, members).astype(jnp.float32)
    summed = jnp.zeros((received.shape[0], features), jnp.float32)
    for member in range(members):
        gate_proj = jnp.dot(received, w_gate[member], preferred_element_type=jnp.float32)
        up_proj = jnp.dot(received, w_up[member], preferred_element_type=jnp.float32)
        activated = (jax.nn.silu(gate_proj) * up_proj).astype(jnp.bfloat16)
        summed = summed + expert_weights[:, member : member + 1] * jnp.dot(
            activated, w_down[member], preferred_element_type=jnp.float32
        )
    partial_value = summed.reshape(groups, tensors, capacity, features)
    pieces = partial_value.astype(jnp.bfloat16).reshape(groups * tensors, capacity, features)
    received_back = lax.all_to_all(
        pieces, ("group", "tensor"), split_axis=0, concat_axis=0, tiled=True
    )
    received_back = received_back.reshape(groups, tensors, capacity, features).astype(jnp.float32)
    node_rows = jnp.sum(received_back, axis=1).astype(jnp.bfloat16)
    mixture = jnp.einsum("rgc,gcd->rd", slot_bf, node_rows, preferred_element_type=jnp.float32)
    return (stream + mixture).astype(jnp.bfloat16)


def solution(mesh):
    placed = (
        P("dp", ("group", "tensor")),
        P(("group", "tensor"), None),
        P(("dp", "group", "tensor"), None),
        P(),
        P(("dp", "group", "tensor"), None),
        P(("dp", "group", "tensor"), None),
        P("group", None, "tensor"),
        P("group", None, "tensor"),
        P("group", "tensor", None),
    )
    return jax.shard_map(
        on_device,
        mesh=mesh,
        in_specs=placed,
        out_specs=P(("dp", "group", "tensor"), None),
        check_vma=False,
    )
```

profile of v0, /device:TPU:0, one launch (start us, length us, event | category | flops | bytes accessed | tf_op | source)
XLA Modules:
  0.0 101.9 jit_solution(6325420256204085334)
XLA Ops:
  6.6 0.8 copy-done
  7.4 5.2 %convolution_convert_fusion = bf16[64,3584]{1,0:T(8,128)(2,1)} fusion(bf16[64,1024]{1,0:T(8,128)(2,1)S(1)} %copy-done, bf16[1024,3584]{1,0:T(8,128)(2,1)} %param.10), kind=kOutput, calls=%fused_computation.3 | convolution fusion | flops 469991424 | bytes 7929856 | tf_op jit(solution)/shard_map/dot_general | solution.py:27
  12.9 0.2 reduce_window_sum.11
  13.1 0.2 convolution_convert_fusion.2
  13.3 7.8 %all_to_all.15 = bf16[4,6,2]{1,2,0:T(2,128)(2,1)S(1)} all-to-all(bf16[4,6,2]{1,2,0:T(2,128)(2,1)S(1)} %convolution_convert_fusion.2), channel_id=1, replica_groups=mesh['dp'=4,'group'=4,'tensor'=2] {'group'}, dimensions={0} | all-to-all | bytes 192 | tf_op jit(solution)/shard_map/all_to_all | solution.py:50
  21.1 0.1 copy.32
  21.2 4.3 %all-gather = bf16[4,12,2]{0,2,1:T(2,128)(2,1)S(1)} all-gather(bf16[4,6,2]{0,2,1:T(2,128)(2,1)S(1)} %copy.32), channel_id=2, replica_groups=mesh['dp'=4,'group'=4,'tensor'=2] {'tensor'}, dimensions={1}, use_global_device_ids=true | all-gather | bytes 288 | tf_op jit(solution)/shard_map/all_gather | solution.py:54
  25.5 0.1 copy.33
  25.6 0.1 reshape.44
  25.7 23.9 %reduce-scatter.2.cloned.1.call-done = bf16[8,3584]{1,0:T(8,128)(2,1)} async-done(((bf16[64,3584]{1,0:T(8,128)(2,1)}), bf16[8,3584]{1,0:T(8,128)(2,1)}) %reduce-scatter.2.cloned.1.call-update) | async-done | bytes 57360 | tf_op jit(solution)/shard_map/reduce_scatter | solution.py:26
  49.6 1.0 fusion.36
  50.6 1.8 %convolution_convert_fusion.1 = bf16[4,6,3584]{2,1,0:T(8,128)(2,1)} fusion(f32[3584]{0:T(1024)S(1)} %copy-done.3, f32[8]{0:T(128)S(1)} %add_rsqrt_fusion, f32[8,4]{0,1:T(4,128)S(1)} %compare_convert_fusion, f32[8,4]{0,1:T(4,128)S(1)} %broadcast_add_fusion, bf16[8,3584]{1,0:T(8,128)(2,1)} %reduce-scatter.2.cloned.1.call-done, bf16[8,3584]{1,0:T(8,128)(2,1)S(1)} %copy-done.1), kind=kOutput, calls=%fused_computation.5 | convolution fusion | flops 1692032 | bytes 301344 | tf_op jit(solution)/shard_map/rgc,rd->gcd/dot_general | solution.py:44
  52.4 3.4 %all-to-all-start.1 = ((bf16[4,6,3584]{2,1,0:T(8,128)(2,1)}), bf16[4,6,3584]{2,1,0:T(8,128)(2,1)S(1)}, u32[]{:S(2)}, u32[]{:S(2)}) async-start(bf16[4,6,3584]{2,1,0:T(8,128)(2,1)} %convolution_convert_fusion.1), calls=%async_computation.2 | async-start | bytes 458752 | tf_op jit(solution)/shard_map/all_to_all | solution.py:49
  55.8 5.6 %all-to-all-done.1 = bf16[4,6,3584]{2,1,0:T(8,128)(2,1)S(1)} async-done(((bf16[4,6,3584]{2,1,0:T(8,128)(2,1)}), bf16[4,6,3584]{2,1,0:T(8,128)(2,1)S(1)}, u32[]{:S(2)}, u32[]{:S(2)}) %all-to-all-start.1) | async-done | bytes 172064 | tf_op jit(solution)/shard_map/all_to_all | solution.py:49
  61.4 0.1 copy.35
  61.5 6.6 %all-gather.1 = bf16[4,12,3584]{2,0,1:T(4,128)(2,1)S(1)} all-gather(bf16[4,6,3584]{2,0,1:T(4,128)(2,1)S(1)} %copy.35), channel_id=3, replica_groups=mesh['dp'=4,'group'=4,'tensor'=2] {'tensor'}, dimensions={1}, use_global_device_ids=true | all-gather | bytes 516096 | tf_op jit(solution)/shard_map/all_gather | solution.py:53
  68.3 2.8 %fusion.7 = f32[48,512]{1,0:T(8,128)S(1)} fusion(bf16[48,3584]{1,0:T(8,128)(2,1)S(1)} %reshape.42, bf16[2,3584,512]{2,1,0:T(8,128)(2,1)} %param.15), kind=kOutput, calls=%fused_computation.12 | convolution fusion | flops 176160768 | bytes 4112384 | tf_op jit(solution)/shard_map/dot_general | solution.py:60
  71.1 2.8 %fusion.12 = f32[48,512]{1,0:T(8,128)S(1)} fusion(bf16[48,3584]{1,0:T(8,128)(2,1)S(1)} %reshape.42, bf16[2,3584,512]{2,1,0:T(8,128)(2,1)} %param.15), kind=kOutput, calls=%fused_computation.17 | convolution fusion | flops 176160768 | bytes 4112384 | tf_op jit(solution)/shard_map/dot_general | solution.py:60
  73.8 4.6 %convolution_multiply_fusion = f32[48,3584]{1,0:T(8,128)S(1)} fusion(bf16[2,512,3584]{2,1,0:T(8,128)(2,1)} %param.17, bf16[48,3584]{1,0:T(8,128)(2,1)S(1)} %reshape.42, bf16[2,3584,512]{2,1,0:T(8,128)(2,1)} %param.16, f32[48]{0:T(128)S(1)} %get-tuple-element.6, f32[48,512]{1,0:T(8,128)S(1)} %fusion.7), kind=kOutput, calls=%fused_computation | convolution fusion | flops 352641024 | bytes 8470720 | tf_op jit(solution)/shard_map/dot_general | solution.py:63
  78.5 4.6 %fusion.1 = bf16[48,3584]{1,0:T(8,128)(2,1)S(1)} fusion(f32[48,3584]{1,0:T(8,128)S(1)} %convolution_multiply_fusion, bf16[2,512,3584]{2,1,0:T(8,128)(2,1)} %param.17, bf16[48,3584]{1,0:T(8,128)(2,1)S(1)} %reshape.42, bf16[2,3584,512]{2,1,0:T(8,128)(2,1)} %param.16, f32[48]{0:T(128)S(1)} %get-tuple-element.5, f32[48,512]{1,0:T(8,128)S(1)} %fusion.12), kind=kOutput, calls=%fused_computation.4 | convolution fusion | flops 352985088 | bytes 8814784 | tf_op jit(solution)/shard_map/dot_general | solution.py:63
  83.1 0.1 convert_element_type.98
  83.2 10.7 %all_to_all.16 = bf16[8,6,3584]{2,1,0:T(8,128)(2,1)S(1)} all-to-all(bf16[8,6,3584]{2,1,0:T(8,128)(2,1)S(1)} %convert_element_type.98), channel_id=1, replica_groups=mesh['dp'=4,'group'=4,'tensor'=2] {'group','tensor'}, dimensions={0} | all-to-all | bytes 688128 | tf_op jit(solution)/shard_map/all_to_all | solution.py:68
  94.0 0.1 bitcast_reduce_fusion
  94.1 1.0 fusion.3
  (23 shorter events, 0.4 us)
Async XLA Ops:
  6.5 0.9 copy-start
  6.5 6.2 %copy-start.5 = (bf16[8,4]{0,1:T(4,128)(2,1)S(1)}, bf16[8,4]{0,1:T(4,128)(2,1)}, u32[]{:S(2)}) copy-start(bf16[8,4]{0,1:T(4,128)(2,1)} %param.14) | copy-start | bytes 196
  6.5 6.2 %copy-start.4 = (s32[8,4]{0,1:T(4,128)S(1)}, s32[8,4]{0,1:T(4,128)}, u32[]{:S(2)}) copy-start(s32[8,4]{0,1:T(4,128)} %param.13) | copy-start | bytes 388
  6.5 43.1 %copy-start.1 = (bf16[8,3584]{1,0:T(8,128)(2,1)S(1)}, bf16[8,3584]{1,0:T(8,128)(2,1)}, u32[]{:S(2)}) copy-start(bf16[8,3584]{1,0:T(8,128)(2,1)} %param.11) | copy-start | bytes 172036
  6.5 44.0 %copy-start.3 = (f32[3584]{0:T(1024)S(1)}, f32[3584]{0:T(1024)}, u32[]{:S(2)}) copy-start(f32[3584]{0:T(1024)} %param.12) | copy-start | bytes 43012
  6.5 43.1 %reduce-scatter.2.cloned.1.call-start = ((), (), s32[]{:S(2)}) async-start(), calls=%async_computation.4 | async-start | bytes 516096 | tf_op jit(solution)/shard_map/reduce_scatter | solution.py:26
  52.4 9.0 %all-to-all-start.1 = ((bf16[4,6,3584]{2,1,0:T(8,128)(2,1)}), bf16[4,6,3584]{2,1,0:T(8,128)(2,1)S(1)}, u32[]{:S(2)}, u32[]{:S(2)}) async-start(bf16[4,6,3584]{2,1,0:T(8,128)(2,1)} %convolution_convert_fusion.1), calls=%async_computation.2 | async-start | bytes 458752 | tf_op jit(solution)/shard_map/all_to_all | solution.py:49
  78.5 15.6 %copy-start.2 = (bf16[8,3584]{1,0:T(8,128)(2,1)S(1)}, bf16[8,3584]{1,0:T(8,128)(2,1)}, u32[]{:S(2)}) copy-start(bf16[8,3584]{1,0:T(8,128)(2,1)} %reduce-scatter.2.cloned.1.call-done) | copy-start | bytes 172036
Sparse Core Ops, SparseCore 0:
  12.8 36.7 reduce-scatter.1
where the time goes:
time: 102 us
  waiting for transfers between devices  29.6 us (29%)
  blocking collectives  29.4 us (29%)
  matrix products  23 us (23%)
  between operations  13.5 us (13%)
  starting transfers between devices  3.42 us (3%)
  local copies, waits for them, and re-layouts  1.62 us (2%)
  other arithmetic  1.36 us (1%)
    reduce_scatter x1, waiting for transfers between devices, on_device(): lax.psum_scatter(jnp.dot(attn_heads, out_proj, preferred_element_type=jnp...  23.9 us
    all_to_all x1, blocking collectives, on_device(): lax.all_to_all(pieces, ('group', 'tensor'), split_axis=0, concat_axis=0,...  10.7 us
    dot_general x2, matrix products, on_device(): jnp.dot(activated, w_down[member], preferred_element_type=jnp.float32)  9.24 us
    all_to_all x1, blocking collectives, on_device(): lax.all_to_all(send_weights, 'group', split_axis=0, concat_axis=0, tiled=...  7.75 us
    all_gather x1, blocking collectives, on_device(): lax.all_gather(arrived[0][:, None], 'tensor', axis=1, tiled=True)  6.59 us
    all_to_all x1, waiting for transfers between devices, on_device(): lax.all_to_all(send_rows, 'group', split_axis=0, concat_axis=0, tiled=True)  5.64 us
    dot_general x2, matrix products, on_device(): jnp.dot(received, w_gate[member], preferred_element_type=jnp.float32)  5.53 us
    dot_general x1, matrix products, on_device(): jnp.dot(attn_heads, out_proj, preferred_element_type=jnp.float32)  5.23 us
  transfers between devices with their start and end apart: 2, of which 2 were waited for; matrix products, arithmetic and copies ran while one was open for 1% of the time, Pallas kernels for 0%

commit v1 on v0

v1 whole, which is shorter than its diff:
```python
import functools

import jax
import jax.numpy as jnp
from jax import lax
from jax.experimental import pallas as pl
from jax.experimental.pallas import tpu as pltpu
from jax.sharding import PartitionSpec as P

MESH = pl.DeviceIdType.MESH
F32 = jnp.float32
BF16 = jnp.bfloat16
META = 128
LAG = 3


def column_chunks(features, most=7):
    for width in (256, 128):
        if features % width == 0:
            tiles = features // width
            return max(n for n in range(1, min(most, tiles) + 1) if tiles % n == 0)
    return 1


def kernel(
    dims,
    attn_hbm, wo_hbm, res_hbm, gain_hbm, ids_hbm, gw_hbm, wg_hbm, wu_hbm, wd_hbm,
    out_hbm,
    attn_v, attn_blocks, attn_p, res_v, gain_v, ids_v, gw_v,
    wo_v, wg_v, wu_v, wd_v,
    keep1, send1, recv1, own2, send2, recv2, hidden_v, square_v,
    rows_own, rows_sib, meta_own, meta_sib,
    acc_gate, acc_up, act_v,
    keep4, send4, recv4, own5, send5, recv5, out_v,
    small_sem, wo_sem, wg_sem, wu_sem, wd_sem, out_sem,
    stage_send, stage_recv,
):
    chunks, width, chips, tensors, rows, members, experts_all = dims
    half = chips * rows
    group, tensor = lax.axis_index("group"), lax.axis_index("tensor")
    high, low = lax.div(group, 2), lax.rem(group, 2)
    place = high * tensors + tensor

    def device(position, side):
        position = lax.rem(position + chips, chips)
        return {"group": lax.div(position, tensors) * 2 + side, "tensor": lax.rem(position, tensors)}

    sibling = {"group": high * 2 + 1 - low, "tensor": tensor}

    barrier = pltpu.get_barrier_semaphore()
    pl.semaphore_signal(barrier, inc=1, device_id=sibling, device_id_type=MESH)
    for offset in range(1, chips):
        pl.semaphore_signal(
            barrier, inc=1, device_id=device(place + offset, low), device_id_type=MESH
        )

    def cols(c):
        return pl.ds(c * width, width)

    smalls = [
        pltpu.make_async_copy(src, dst, small_sem.at[i])
        for i, (src, dst) in enumerate(
            [(attn_hbm, attn_v), (res_hbm, res_v), (gain_hbm, gain_v), (ids_hbm, ids_v), (gw_hbm, gw_v)]
        )
    ]
    wo_copies = [
        pltpu.make_async_copy(wo_hbm.at[:, cols(c)], wo_v.at[c], wo_sem.at[c]) for c in range(chunks)
    ]
    wg_copies = [
        pltpu.make_async_copy(wg_hbm.at[:, cols(c), :], wg_v.at[c], wg_sem.at[c])
        for c in range(chunks)
    ]
    wu_copies = [
        pltpu.make_async_copy(wu_hbm.at[:, cols(c), :], wu_v.at[c], wu_sem.at[c])
        for c in range(chunks)
    ]
    wd_copies = [
        pltpu.make_async_copy(wd_hbm.at[:, :, cols(c)], wd_v.at[c], wd_sem.at[c])
        for c in range(chunks)
    ]
    smalls[0].start()
    wo_copies[0].start()
    for copy in smalls[1:]:
        copy.start()
    for copy in wo_copies[1:]:
        copy.start()
    for c in range(chunks):
        wg_copies[c].start()
        wu_copies[c].start()
    for copy in wd_copies:
        copy.start()

    def wait_bytes(ref, sem):
        pltpu.make_async_copy(ref, ref, sem).wait()

    def to_sibling(stage, c, src, dst):
        pltpu.make_async_remote_copy(
            src_ref=src, dst_ref=dst, send_sem=stage_send.at[stage, c],
            recv_sem=stage_recv.at[stage, c], device_id=sibling, device_id_type=MESH,
        ).start()

    def to_owners(stage, c, src, dst):
        for offset in range(1, chips):
            pltpu.make_async_remote_copy(
                src_ref=src.at[offset - 1], dst_ref=dst.at[offset - 1],
                send_sem=stage_send.at[stage, c], recv_sem=stage_recv.at[stage, c],
                device_id=device(place - offset, low), device_id_type=MESH,
            ).start()

    def to_chips(stage, c, block):
        for offset in range(1, chips):
            pltpu.make_async_remote_copy(
                src_ref=block.at[0], dst_ref=block.at[offset],
                send_sem=stage_send.at[stage, c], recv_sem=stage_recv.at[stage, c],
                device_id=device(place + offset, low), device_id_type=MESH,
            ).start()

    def peers(block):
        return block.at[pl.ds(1, chips - 1)]

    smalls[0].wait()
    attn_blocks[...] = attn_v[...].astype(F32).reshape(attn_blocks.shape)
    picked = []
    for side in (low, 1 - low):
        for offset in range(chips):
            position = lax.rem(place - offset + chips, chips)
            owner = (lax.div(position, tensors) * 2 + side) * tensors + lax.rem(position, tensors)
            picked.append(attn_blocks[owner])
    attn_p[...] = jnp.concatenate(picked, axis=0).astype(BF16)

    def split(product, keep, send):
        keep[...] = product[:half].reshape(chips, rows, width)
        send[...] = product[half:].reshape(chips, rows, width).astype(BF16)

    def project(c):
        wo_copies[c].wait()
        product = jnp.dot(attn_p[...], wo_v[c], preferred_element_type=F32)
        split(product, keep1.at[c], send1.at[c])
        if c == 0:
            pl.semaphore_wait(barrier, chips)
        to_sibling(0, c, send1.at[c], recv1.at[c])

    def add_sibling(c):
        wait_bytes(recv1.at[c], stage_recv.at[0, c])
        total = keep1[c] + recv1[c].astype(F32)
        own2[c] = total[0]
        send2[c] = total[1:].astype(BF16)
        to_owners(1, c, send2.at[c], recv2.at[c])

    def finish_hidden(c):
        wait_bytes(recv2.at[c], stage_recv.at[1, c])
        if c == 0:
            for copy in smalls[1:]:
                copy.wait()
        total = own2[c] + jnp.sum(recv2[c].astype(F32), axis=0)
        here = slice(c * width, (c + 1) * width)
        projected = total.astype(BF16).astype(F32)
        hidden = (res_v[:, here].astype(F32) + projected).astype(BF16).astype(F32)
        hidden_v[c] = hidden
        square_v[...] = hidden * hidden if c == 0 else square_v[...] + hidden * hidden
        rows_own[c, 0] = (hidden * gain_v[:, here]).astype(BF16)
        to_chips(2, c, rows_own.at[c])
        if c == chunks - 1:
            send_meta()

    def send_meta():
        mean = jnp.sum(square_v[...], axis=1, keepdims=True) / (chunks * width)
        scale = lax.rsqrt(mean + 1e-06)
        lane = lax.broadcasted_iota(jnp.int32, (rows, META), 1)
        ids = ids_v[...]
        weights = gw_v[...].astype(F32)
        block = jnp.where(lane == experts_all, scale, 0.0)
        for k in range(ids.shape[1]):
            block = block + jnp.where(lane == ids[:, k : k + 1], weights[:, k : k + 1], 0.0)
        meta_own[0] = block
        to_chips(2, chunks, meta_own)

    def forward(c):
        wait_bytes(peers(rows_own.at[c]), stage_recv.at[2, c])
        to_sibling(3, c, rows_own.at[c], rows_sib.at[c])
        if c == chunks - 1:
            wait_bytes(peers(meta_own), stage_recv.at[2, chunks])
            to_sibling(3, chunks, meta_own, meta_sib)

    def experts(c):
        wg_copies[c].wait()
        wu_copies[c].wait()
        wait_bytes(rows_sib.at[c], stage_recv.at[3, c])
        both = jnp.concatenate(
            [rows_own[c].astype(F32).reshape(half, width), rows_sib[c].astype(F32).reshape(half, width)],
            axis=0,
        ).astype(BF16)
        for member in range(members):
            gate = jnp.dot(both, wg_v[c, member], preferred_element_type=F32)
            up = jnp.dot(both, wu_v[c, member], preferred_element_type=F32)
            acc_gate[member] = gate if c == 0 else acc_gate[member] + gate
            acc_up[member] = up if c == 0 else acc_up[member] + up

    def activate():
        wait_bytes(meta_sib, stage_recv.at[3, chunks])
        block = jnp.concatenate([meta_own[...].reshape(half, META), meta_sib[...].reshape(half, META)], axis=0)
        lane = lax.broadcasted_iota(jnp.int32, block.shape, 1)
        scale = block[:, experts_all : experts_all + 1]
        for member in range(members):
            weight = jnp.sum(
                jnp.where(lane == group * members + member, block, 0.0), axis=1, keepdims=True
            )
            gate = acc_gate[member] * scale
            up = acc_up[member] * scale
            act_v[member] = (gate / (1.0 + jnp.exp(-gate)) * up * weight).astype(BF16)

    def down(c):
        wd_copies[c].wait()
        product = jnp.dot(act_v[0], wd_v[c, 0], preferred_element_type=F32)
        for member in range(1, members):
            product = product + jnp.dot(act_v[member], wd_v[c, member], preferred_element_type=F32)
        split(product, keep4.at[c], send4.at[c])
        to_sibling(4, c, send4.at[c], recv4.at[c])

    def add_sibling_down(c):
        wait_bytes(recv4.at[c], stage_recv.at[4, c])
        total = keep4[c] + recv4[c].astype(F32)
        own5[c] = total[0]
        send5[c] = total[1:].astype(BF16)
        to_owners(5, c, send5.at[c], recv5.at[c])

    def finish(c):
        wait_bytes(recv5.at[c], stage_recv.at[5, c])
        total = own5[c] + jnp.sum(recv5[c].astype(F32), axis=0)
        out_v[c] = (hidden_v[c] + total).astype(BF16)
        pltpu.make_async_copy(out_v.at[c], out_hbm.at[:, cols(c)], out_sem.at[c]).start()

    def pipeline(stages):
        steps = [(c + LAG * s, -s, c, stage) for s, stage in enumerate(stages) for c in range(chunks)]
        for _, _, c, stage in sorted(steps, key=lambda step: step[:3]):
            stage(c)

    pipeline([project, add_sibling, finish_hidden, forward, experts])
    activate()
    pipeline([down, add_sibling_down, finish])

    for c in range(chunks):
        pltpu.make_async_copy(out_v.at[c], out_hbm.at[:, cols(c)], out_sem.at[c]).wait()
        wait_bytes(send1.at[c], stage_send.at[0, c])
        wait_bytes(send2.at[c], stage_send.at[1, c])
        wait_bytes(peers(rows_own.at[c]), stage_send.at[2, c])
        wait_bytes(rows_own.at[c], stage_send.at[3, c])
        wait_bytes(send4.at[c], stage_send.at[4, c])
        wait_bytes(send5.at[c], stage_send.at[5, c])
    wait_bytes(peers(meta_own), stage_send.at[2, chunks])
    wait_bytes(meta_own, stage_send.at[3, chunks])


def on_device(
    attn_heads, out_proj, residual_in, norm_gain, expert_ids, gate_weights, w_gate, w_up, w_down
):
    rows, features = residual_in.shape
    tokens, heads = attn_heads.shape
    groups = lax.axis_size("group")
    tensors = lax.axis_size("tensor")
    members, _, units = w_gate.shape
    chips = groups // 2 * tensors
    experts_all = groups * members
    chunks = column_chunks(features)
    width = features // chunks
    dims = (chunks, width, chips, tensors, rows, members, experts_all)

    def vmem(shape, dtype):
        return pltpu.VMEM(shape, dtype)

    exchange = [
        vmem((chunks, chips, rows, width), F32),
        vmem((chunks, chips, rows, width), BF16),
        vmem((chunks, chips, rows, width), BF16),
        vmem((chunks, rows, width), F32),
        vmem((chunks, chips - 1, rows, width), BF16),
        vmem((chunks, chips - 1, rows, width), BF16),
    ]
    scratch = [
        vmem((tokens, heads), BF16),
        vmem((tokens // rows, rows, heads), F32),
        vmem((tokens, heads), BF16),
        vmem((rows, features), BF16),
        vmem((1, features), F32),
        vmem(expert_ids.shape, expert_ids.dtype),
        vmem(gate_weights.shape, gate_weights.dtype),
        vmem((chunks, heads, width), BF16),
        vmem((chunks, members, width, units), BF16),
        vmem((chunks, members, width, units), BF16),
        vmem((chunks, members, units, width), BF16),
        *exchange,
        vmem((chunks, rows, width), F32),
        vmem((rows, width), F32),
        vmem((chunks, chips, rows, width), BF16),
        vmem((chunks, chips, rows, width), BF16),
        vmem((chips, rows, META), F32),
        vmem((chips, rows, META), F32),
        vmem((members, tokens, units), F32),
        vmem((members, tokens, units), F32),
        vmem((members, tokens, units), BF16),
        *exchange,
        vmem((chunks, rows, width), BF16),
        pltpu.SemaphoreType.DMA((5,)),
        pltpu.SemaphoreType.DMA((chunks,)),
        pltpu.SemaphoreType.DMA((chunks,)),
        pltpu.SemaphoreType.DMA((chunks,)),
        pltpu.SemaphoreType.DMA((chunks,)),
        pltpu.SemaphoreType.DMA((chunks,)),
        pltpu.SemaphoreType.DMA((6, chunks + 1)),
        pltpu.SemaphoreType.DMA((6, chunks + 1)),
    ]
    weights = out_proj.size + w_gate.size + w_up.size + w_down.size
    return pl.pallas_call(
        functools.partial(kernel, dims),
        out_shape=jax.ShapeDtypeStruct((rows, features), BF16),
        in_specs=[pl.BlockSpec(memory_space=pl.ANY)] * 9,
        out_specs=pl.BlockSpec(memory_space=pl.ANY),
        scratch_shapes=scratch,
        cost_estimate=pl.CostEstimate(
            flops=2 * tokens * weights, bytes_accessed=2 * weights, transcendentals=0
        ),
        compiler_params=pltpu.CompilerParams(
            collective_id=0, has_side_effects=True, vmem_limit_bytes=56 * 1024 * 1024
        ),
        name="projected_experts",
    )(
        attn_heads, out_proj, residual_in, norm_gain.reshape(1, features),
        expert_ids, gate_weights, w_gate, w_up, w_down,
    )


def solution(mesh):
    placed = (
        P("dp", ("group", "tensor")),
        P(("group", "tensor"), None),
        P(("dp", "group", "tensor"), None),
        P(),
        P(("dp", "group", "tensor"), None),
        P(("dp", "group", "tensor"), None),
        P("group", None, "tensor"),
        P("group", None, "tensor"),
        P("group", "tensor", None),
    )
    return jax.shard_map(
        on_device,
        mesh=mesh,
        in_specs=placed,
        out_specs=P(("dp", "group", "tensor"), None),
        check_vma=False,
    )
```

time: 102 us -> 40.3 us (0.40)
  Pallas kernels: 0 us -> 34.5 us
  waiting for transfers between devices: 29.6 us -> 0 us
  blocking collectives: 29.4 us -> 0 us
  matrix products: 23 us -> 0 us
  between operations: 13.5 us -> 0.01 us
  local copies, waits for them, and re-layouts: 1.62 us -> 5.45 us
  starting transfers between devices: 3.42 us -> 0 us
  other arithmetic: 1.36 us -> 0 us
    pallas_call x0 -> x1, Pallas kernels: none -> 34.5 us  [on_device(): pl.pallas_call(functools.partial(kernel, dims), out_shape=jax.ShapeDtypeS...]
    reduce_scatter x1 -> x0, waiting for transfers between devices: 23.9 us -> none  [on_device(): lax.psum_scatter(jnp.dot(attn_heads, out_proj, preferred_element_type=jnp...]
    dot_general x8 -> x0, matrix products: 23 us -> none  [the longest x2 9.24 us: on_device(): jnp.dot(activated, w_down[member], preferred_element_type=jnp.float32)]
    all_to_all x2 -> x0, blocking collectives: 18.5 us -> none  [the longest x1 10.7 us: on_device(): lax.all_to_all(pieces, ('group', 'tensor'), split_axis=0, concat_axis=0,...]
    all_gather x2 -> x0, blocking collectives: 10.9 us -> none  [the longest x1 6.59 us: on_device(): lax.all_gather(arrived[0][:, None], 'tensor', axis=1, tiled=True)]
    all_to_all x1 -> x0, waiting for transfers between devices: 5.64 us -> none  [on_device(): lax.all_to_all(send_rows, 'group', split_axis=0, concat_axis=0, tiled=True)]
    all_to_all x1 -> x0, starting transfers between devices: 3.38 us -> none  [on_device(): lax.all_to_all(send_rows, 'group', split_axis=0, concat_axis=0, tiled=True)]
    unnamed x12 -> x3, local copies, waits for them, and re-layouts: 0.87 us -> 4.12 us
  transfers between devices with their start and end apart: 2 -> 0, of which waited for: 2 -> 0; matrix products, arithmetic and copies ran while one was open for 1% -> 0% of each run, Pallas kernels for 0% -> 0%
where the time goes in v1:
time: 40.3 us; the launch traced here: 40 us
  Pallas kernels  34.5 us (86%)
  local copies, waits for them, and re-layouts  5.45 us (14%)
    pallas_call x1, Pallas kernels, on_device(): pl.pallas_call(functools.partial(kernel, dims), out_shape=jax.ShapeDtypeS...  34.5 us
    unnamed x3, local copies, waits for them, and re-layouts  4.12 us
    reshape x1, local copies, waits for them, and re-layouts, on_device(): norm_gain.reshape(1, features)  1.33 us

profile of v1, /device:TPU:0, one launch (start us, length us, event | category | flops | bytes accessed | tf_op | source)
XLA Modules:
  0.0 40.0 jit_solution(6648616649543948749)
XLA Ops:
  0.0 1.3 %copy.11.gw_hbm = bf16[8,4]{1,0:T(8,128)(2,1)} copy(bf16[8,4]{0,1:T(4,128)(2,1)} %param.14) | data formatting | bytes 128 | tf_op args[5]
  1.3 1.3 %copy.10.ids_hbm = s32[8,4]{1,0:T(8,128)} copy(s32[8,4]{0,1:T(4,128)} %param.13) | data formatting | bytes 256 | tf_op args[4]
  2.7 1.3 %reshape.3.gain_hbm = f32[1,3584]{1,0:T(1,128)} reshape(f32[3584]{0:T(1024)} %param.12) | data formatting | bytes 28672 | tf_op jit(solution)/shard_map/reshape | solution.py:327
  4.0 34.5 %projected_experts.1 = bf16[8,3584]{1,0:T(8,128)(2,1)} custom-call(bf16[64,1024]{1,0:T(8,128)(2,1)} %attn_hbm.1, bf16[1024,3584]{1,0:T(8,128)(2,1)} %wo_hbm.1, bf16[8,3584]{1,0:T(8,128)(2,1)} %res_hbm.1, f32[1,3584]{1,0:T(1,128)} %reshape.3.gain_hbm, s32[8,4]{1,0:T(8,128)} %copy.10.ids_hbm, bf16[8,4]{1,0:T(8,128)(2,1)} %copy.11.gw_hbm, ...), custom_call_target="tpu_custom_call" | custom-call | flops 1879048192 | bytes 29360128 | tf_op jit(solution)/shard_map/projected_experts/pallas_call | solution.py:313
  38.6 1.4 %copy.13 = bf16[8,3584]{1,0:T(8,128)(2,1)} copy(bf16[8,3584]{1,0:T(8,128)(2,1)} %projected_experts.1) | data formatting | bytes 114688

commit v2 on v1

--- a/solution.py
+++ b/solution.py
@@ -11,7 +11,7 @@
 F32 = jnp.float32
 BF16 = jnp.bfloat16
 META = 128
-LAG = 3
+LAGS = (0, 4, 10, 17, 21)
 
 
 def column_chunks(features, most=7):
@@ -28,7 +28,7 @@
     out_hbm,
     attn_v, attn_blocks, attn_p, res_v, gain_v, ids_v, gw_v,
     wo_v, wg_v, wu_v, wd_v,
-    keep1, send1, recv1, own2, send2, recv2, hidden_v, square_v,
+    keep1, send1, recv1, own2, send2, recv2, hidden_v, square_v, table_v,
     rows_own, rows_sib, meta_own, meta_sib,
     acc_gate, acc_up, act_v,
     keep4, send4, recv4, own5, send5, recv5, out_v,
@@ -139,6 +139,8 @@
         if c == 0:
             pl.semaphore_wait(barrier, chips)
         to_sibling(0, c, send1.at[c], recv1.at[c])
+        if c == chunks - 1:
+            routing_table()
 
     def add_sibling(c):
         wait_bytes(recv1.at[c], stage_recv.at[0, c])
@@ -149,30 +151,37 @@
 
     def finish_hidden(c):
         wait_bytes(recv2.at[c], stage_recv.at[1, c])
-        if c == 0:
-            for copy in smalls[1:]:
-                copy.wait()
         total = own2[c] + jnp.sum(recv2[c].astype(F32), axis=0)
         here = slice(c * width, (c + 1) * width)
         projected = total.astype(BF16).astype(F32)
         hidden = (res_v[:, here].astype(F32) + projected).astype(BF16).astype(F32)
         hidden_v[c] = hidden
         square_v[...] = hidden * hidden if c == 0 else square_v[...] + hidden * hidden
-        rows_own[c, 0] = (hidden * gain_v[:, here]).astype(BF16)
+        rows_own[c, 0] = (hidden * gain_v[here][None]).astype(BF16)
         to_chips(2, c, rows_own.at[c])
         if c == chunks - 1:
             send_meta()
+
+    def routing_table():
+        for copy in smalls[1:]:
+            copy.wait()
+        lane = lax.broadcasted_iota(jnp.int32, (rows, META), 1).astype(F32)
+        square = (rows, rows)
+        diagonal = lax.broadcasted_iota(jnp.int32, square, 0) == lax.broadcasted_iota(jnp.int32, square, 1)
+        ids = ids_v[...].astype(F32)
+        weights = gw_v[...].astype(F32)
+        block = jnp.zeros((rows, META), F32)
+        for k in range(ids.shape[0]):
+            expert = jnp.sum(jnp.where(diagonal, ids[k : k + 1], 0.0), axis=1, keepdims=True)
+            weight = jnp.sum(jnp.where(diagonal, weights[k : k + 1], 0.0), axis=1, keepdims=True)
+            block = block + jnp.where(lane == expert, weight, 0.0)
+        table_v[...] = block
 
     def send_meta():
         mean = jnp.sum(square_v[...], axis=1, keepdims=True) / (chunks * width)
         scale = lax.rsqrt(mean + 1e-06)
         lane = lax.broadcasted_iota(jnp.int32, (rows, META), 1)
-        ids = ids_v[...]
-        weights = gw_v[...].astype(F32)
-        block = jnp.where(lane == experts_all, scale, 0.0)
-        for k in range(ids.shape[1]):
-            block = block + jnp.where(lane == ids[:, k : k + 1], weights[:, k : k + 1], 0.0)
-        meta_own[0] = block
+        meta_own[0] = jnp.where(lane == experts_all, scale, table_v[...])
         to_chips(2, chunks, meta_own)
 
     def forward(c):
@@ -231,7 +240,7 @@
         pltpu.make_async_copy(out_v.at[c], out_hbm.at[:, cols(c)], out_sem.at[c]).start()
 
     def pipeline(stages):
-        steps = [(c + LAG * s, -s, c, stage) for s, stage in enumerate(stages) for c in range(chunks)]
+        steps = [(c + LAGS[s], s, c, stage) for s, stage in enumerate(stages) for c in range(chunks)]
         for _, _, c, stage in sorted(steps, key=lambda step: step[:3]):
             stage(c)
 
@@ -281,9 +290,9 @@
         vmem((tokens // rows, rows, heads), F32),
         vmem((tokens, heads), BF16),
         vmem((rows, features), BF16),
-        vmem((1, features), F32),
-        vmem(expert_ids.shape, expert_ids.dtype),
-        vmem(gate_weights.shape, gate_weights.dtype),
+        vmem((features,), F32),
+        vmem(expert_ids.shape[::-1], expert_ids.dtype),
+        vmem(gate_weights.shape[::-1], gate_weights.dtype),
         vmem((chunks, heads, width), BF16),
         vmem((chunks, members, width, units), BF16),
         vmem((chunks, members, width, units), BF16),
@@ -291,6 +300,7 @@
         *exchange,
         vmem((chunks, rows, width), F32),
         vmem((rows, width), F32),
+        vmem((rows, META), F32),
         vmem((chunks, chips, rows, width), BF16),
         vmem((chunks, chips, rows, width), BF16),
         vmem((chips, rows, META), F32),
@@ -324,8 +334,8 @@
         ),
         name="projected_experts",
     )(
-        attn_heads, out_proj, residual_in, norm_gain.reshape(1, features),
-        expert_ids, gate_weights, w_gate, w_up, w_down,
+        attn_heads, out_proj, residual_in, norm_gain,
+        expert_ids.T, gate_weights.T, w_gate, w_up, w_down,
     )
 
 

time: 40.3 us -> 31.4 us (0.78)
  Pallas kernels: 34.5 us -> 29.8 us
  local copies, waits for them, and re-layouts: 5.45 us -> 1.45 us
    pallas_call x1, Pallas kernels: 34.5 us -> 29.8 us  [on_device(): pl.pallas_call(functools.partial(kernel, dims), out_shape=jax.ShapeDtypeS...]
    unnamed x3 -> x1, local copies, waits for them, and re-layouts: 4.12 us -> 1.45 us
    reshape x1 -> x0, local copies, waits for them, and re-layouts: 1.33 us -> none  [on_device(): norm_gain.reshape(1, features)]
where the time goes in v2:
time: 31.4 us; the launch traced here: 31.2 us
  Pallas kernels  29.8 us (95%)
  local copies, waits for them, and re-layouts  1.45 us (5%)
    pallas_call x1, Pallas kernels, on_device(): pl.pallas_call(functools.partial(kernel, dims), out_shape=jax.ShapeDtypeS...  29.8 us
    unnamed x1, local copies, waits for them, and re-layouts  1.45 us

profile of v2, /device:TPU:0, one launch (start us, length us, event | category | flops | bytes accessed | tf_op | source)
XLA Modules:
  0.0 31.2 jit_solution(10002810141590205008)
XLA Ops:
  0.0 29.8 %projected_experts.1 = bf16[8,3584]{1,0:T(8,128)(2,1)} custom-call(bf16[64,1024]{1,0:T(8,128)(2,1)} %attn_hbm.1, bf16[1024,3584]{1,0:T(8,128)(2,1)} %wo_hbm.1, bf16[8,3584]{1,0:T(8,128)(2,1)} %res_hbm.1, f32[3584]{0:T(1024)} %gain_hbm.1, s32[4,8]{1,0:T(4,128)} %bitcast.2, bf16[4,8]{1,0:T(4,128)(2,1)} %bitcast.3, bf16[2,3584,512]{2,1,0:T(8,128)(2,1)} %wg_hbm.1, ...), custom_call_target="tpu_custom_call" | custom-call | flops 1879048192 | bytes 29360128 | tf_op jit(solution)/shard_map/projected_experts/pallas_call | solution.py:323
  29.8 1.4 %copy.11 = bf16[8,3584]{1,0:T(8,128)(2,1)} copy(bf16[8,3584]{1,0:T(8,128)(2,1)} %projected_experts.1) | data formatting | bytes 114688

commit v3 on v2

--- a/solution.py
+++ b/solution.py
@@ -10,16 +10,19 @@
 MESH = pl.DeviceIdType.MESH
 F32 = jnp.float32
 BF16 = jnp.bfloat16
+UNITS = 4
 META = 128
 LAGS = (0, 4, 10, 17, 21)
 
 
-def column_chunks(features, most=7):
-    for width in (256, 128):
-        if features % width == 0:
-            tiles = features // width
-            return max(n for n in range(1, min(most, tiles) + 1) if tiles % n == 0)
-    return 1
+def column_chunks(features, units, first_short):
+    tile = 256 if features % 256 == 0 else 128
+    count = features // tile
+    sizes = [units] * (count // units) + ([count % units] if count % units else [])
+    if first_short:
+        sizes = sizes[::-1]
+    starts = [sum(sizes[:i]) for i in range(len(sizes))]
+    return tuple((start * tile, size * tile) for start, size in zip(starts, sizes))
 
 
 def kernel(
@@ -28,14 +31,16 @@
     out_hbm,
     attn_v, attn_blocks, attn_p, res_v, gain_v, ids_v, gw_v,
     wo_v, wg_v, wu_v, wd_v,
-    keep1, send1, recv1, own2, send2, recv2, hidden_v, square_v, table_v,
+    keep1, send1, recv1, own2, send2, recv2, hidden_v, table_v,
     rows_own, rows_sib, meta_own, meta_sib,
     acc_gate, acc_up, act_v,
     keep4, send4, recv4, own5, send5, recv5, out_v,
     small_sem, wo_sem, wg_sem, wu_sem, wd_sem, out_sem,
     stage_send, stage_recv,
 ):
-    chunks, width, chips, tensors, rows, members, experts_all = dims
+    spans, down_spans, chips, tensors, rows, members, experts_all = dims
+    chunks, down_chunks = len(spans), len(down_spans)
+    features = res_v.shape[1]
     half = chips * rows
     group, tensor = lax.axis_index("group"), lax.axis_index("tensor")
     high, low = lax.div(group, 2), lax.rem(group, 2)
@@ -54,8 +59,10 @@
             barrier, inc=1, device_id=device(place + offset, low), device_id_type=MESH
         )
 
-    def cols(c):
-        return pl.ds(c * width, width)
+    def part(ref, span, axis=-1):
+        index = [slice(None)] * len(ref.shape)
+        index[axis] = pl.ds(*span)
+        return ref.at[tuple(index)]
 
     smalls = [
         pltpu.make_async_copy(src, dst, small_sem.at[i])
@@ -63,21 +70,16 @@
             [(attn_hbm, attn_v), (res_hbm, res_v), (gain_hbm, gain_v), (ids_hbm, ids_v), (gw_hbm, gw_v)]
         )
     ]
-    wo_copies = [
-        pltpu.make_async_copy(wo_hbm.at[:, cols(c)], wo_v.at[c], wo_sem.at[c]) for c in range(chunks)
-    ]
-    wg_copies = [
-        pltpu.make_async_copy(wg_hbm.at[:, cols(c), :], wg_v.at[c], wg_sem.at[c])
-        for c in range(chunks)
-    ]
-    wu_copies = [
-        pltpu.make_async_copy(wu_hbm.at[:, cols(c), :], wu_v.at[c], wu_sem.at[c])
-        for c in range(chunks)
-    ]
-    wd_copies = [
-        pltpu.make_async_copy(wd_hbm.at[:, :, cols(c)], wd_v.at[c], wd_sem.at[c])
-        for c in range(chunks)
-    ]
+    def fetches(src, dst, sems, pieces, axis):
+        return [
+            pltpu.make_async_copy(part(src, span, axis), part(dst, span, axis), sems.at[c])
+            for c, span in enumerate(pieces)
+        ]
+
+    wo_copies = fetches(wo_hbm, wo_v, wo_sem, spans, 1)
+    wg_copies = fetches(wg_hbm, wg_v, wg_sem, spans, 1)
+    wu_copies = fetches(wu_hbm, wu_v, wu_sem, spans, 1)
+    wd_copies = fetches(wd_hbm, wd_v, wd_sem, down_spans, 2)
     smalls[0].start()
     wo_copies[0].start()
     for copy in smalls[1:]:
@@ -129,36 +131,38 @@
     attn_p[...] = jnp.concatenate(picked, axis=0).astype(BF16)
 
     def split(product, keep, send):
+        width = product.shape[1]
         keep[...] = product[:half].reshape(chips, rows, width)
         send[...] = product[half:].reshape(chips, rows, width).astype(BF16)
 
-    def project(c):
+    def project(c, span):
         wo_copies[c].wait()
-        product = jnp.dot(attn_p[...], wo_v[c], preferred_element_type=F32)
-        split(product, keep1.at[c], send1.at[c])
+        product = jnp.dot(attn_p[...], part(wo_v, span)[...], preferred_element_type=F32)
+        split(product, part(keep1, span), part(send1, span))
         if c == 0:
             pl.semaphore_wait(barrier, chips)
-        to_sibling(0, c, send1.at[c], recv1.at[c])
+        to_sibling(0, c, part(send1, span), part(recv1, span))
         if c == chunks - 1:
             routing_table()
 
-    def add_sibling(c):
-        wait_bytes(recv1.at[c], stage_recv.at[0, c])
-        total = keep1[c] + recv1[c].astype(F32)
-        own2[c] = total[0]
-        send2[c] = total[1:].astype(BF16)
-        to_owners(1, c, send2.at[c], recv2.at[c])
-
-    def finish_hidden(c):
-        wait_bytes(recv2.at[c], stage_recv.at[1, c])
-        total = own2[c] + jnp.sum(recv2[c].astype(F32), axis=0)
-        here = slice(c * width, (c + 1) * width)
+    def add_sibling(c, span):
+        wait_bytes(part(recv1, span), stage_recv.at[0, c])
+        total = part(keep1, span)[...] + part(recv1, span)[...].astype(F32)
+        part(own2, span)[...] = total[0]
+        part(send2, span)[...] = total[1:].astype(BF16)
+        to_owners(1, c, part(send2, span), part(recv2, span))
+
+    squares = []
+
+    def finish_hidden(c, span):
+        wait_bytes(part(recv2, span), stage_recv.at[1, c])
+        total = part(own2, span)[...] + jnp.sum(part(recv2, span)[...].astype(F32), axis=0)
         projected = total.astype(BF16).astype(F32)
-        hidden = (res_v[:, here].astype(F32) + projected).astype(BF16).astype(F32)
-        hidden_v[c] = hidden
-        square_v[...] = hidden * hidden if c == 0 else square_v[...] + hidden * hidden
-        rows_own[c, 0] = (hidden * gain_v[here][None]).astype(BF16)
-        to_chips(2, c, rows_own.at[c])
+        hidden = (part(res_v, span)[...].astype(F32) + projected).astype(BF16).astype(F32)
+        part(hidden_v, span)[...] = hidden
+        part(rows_own, span)[0] = (hidden * part(gain_v, span)[...][None]).astype(BF16)
+        to_chips(2, c, part(rows_own, span))
+        squares.append(jnp.sum(hidden * hidden, axis=1, keepdims=True))
         if c == chunks - 1:
             send_meta()
 
@@ -178,30 +182,29 @@
         table_v[...] = block
 
     def send_meta():
-        mean = jnp.sum(square_v[...], axis=1, keepdims=True) / (chunks * width)
+        mean = sum(squares[1:], squares[0]) / features
         scale = lax.rsqrt(mean + 1e-06)
         lane = lax.broadcasted_iota(jnp.int32, (rows, META), 1)
         meta_own[0] = jnp.where(lane == experts_all, scale, table_v[...])
         to_chips(2, chunks, meta_own)
 
-    def forward(c):
-        wait_bytes(peers(rows_own.at[c]), stage_recv.at[2, c])
-        to_sibling(3, c, rows_own.at[c], rows_sib.at[c])
+    def forward(c, span):
+        wait_bytes(peers(part(rows_own, span)), stage_recv.at[2, c])
+        to_sibling(3, c, part(rows_own, span), part(rows_sib, span))
         if c == chunks - 1:
             wait_bytes(peers(meta_own), stage_recv.at[2, chunks])
             to_sibling(3, chunks, meta_own, meta_sib)
 
-    def experts(c):
+    def experts(c, span):
         wg_copies[c].wait()
         wu_copies[c].wait()
-        wait_bytes(rows_sib.at[c], stage_recv.at[3, c])
+        wait_bytes(part(rows_sib, span), stage_recv.at[3, c])
         both = jnp.concatenate(
-            [rows_own[c].astype(F32).reshape(half, width), rows_sib[c].astype(F32).reshape(half, width)],
-            axis=0,
+            [part(ref, span)[...].astype(F32).reshape(half, span[1]) for ref in (rows_own, rows_sib)], axis=0
         ).astype(BF16)
         for member in range(members):
-            gate = jnp.dot(both, wg_v[c, member], preferred_element_type=F32)
-            up = jnp.dot(both, wu_v[c, member], preferred_element_type=F32)
+            gate = jnp.dot(both, part(wg_v, span, 1)[member], preferred_element_type=F32)
+            up = jnp.dot(both, part(wu_v, span, 1)[member], preferred_element_type=F32)
             acc_gate[member] = gate if c == 0 else acc_gate[member] + gate
             acc_up[member] = up if c == 0 else acc_up[member] + up
 
@@ -218,44 +221,53 @@
             up = acc_up[member] * scale
             act_v[member] = (gate / (1.0 + jnp.exp(-gate)) * up * weight).astype(BF16)
 
-    def down(c):
+    def down(c, span):
         wd_copies[c].wait()
-        product = jnp.dot(act_v[0], wd_v[c, 0], preferred_element_type=F32)
+        product = jnp.dot(act_v[0], part(wd_v, span)[0], preferred_element_type=F32)
         for member in range(1, members):
-            product = product + jnp.dot(act_v[member], wd_v[c, member], preferred_element_type=F32)
-        split(product, keep4.at[c], send4.at[c])
-        to_sibling(4, c, send4.at[c], recv4.at[c])
-
-    def add_sibling_down(c):
-        wait_bytes(recv4.at[c], stage_recv.at[4, c])
-        total = keep4[c] + recv4[c].astype(F32)
-        own5[c] = total[0]
-        send5[c] = total[1:].astype(BF16)
-        to_owners(5, c, send5.at[c], recv5.at[c])
-
-    def finish(c):
-        wait_bytes(recv5.at[c], stage_recv.at[5, c])
-        total = own5[c] + jnp.sum(recv5[c].astype(F32), axis=0)
-        out_v[c] = (hidden_v[c] + total).astype(BF16)
-        pltpu.make_async_copy(out_v.at[c], out_hbm.at[:, cols(c)], out_sem.at[c]).start()
-
-    def pipeline(stages):
-        steps = [(c + LAGS[s], s, c, stage) for s, stage in enumerate(stages) for c in range(chunks)]
+            product = product + jnp.dot(act_v[member], part(wd_v, span)[member], preferred_element_type=F32)
+        split(product, part(keep4, span), part(send4, span))
+        to_sibling(4, c, part(send4, span), part(recv4, span))
+
+    def add_sibling_down(c, span):
+        wait_bytes(part(recv4, span), stage_recv.at[4, c])
+        total = part(keep4, span)[...] + part(recv4, span)[...].astype(F32)
+        part(own5, span)[...] = total[0]
+        part(send5, span)[...] = total[1:].astype(BF16)
+        to_owners(5, c, part(send5, span), part(recv5, span))
+
+    def write_out(c, span):
+        return pltpu.make_async_copy(part(out_v, span), part(out_hbm, span), out_sem.at[c])
+
+    def finish(c, span):
+        wait_bytes(part(recv5, span), stage_recv.at[5, c])
+        total = part(own5, span)[...] + jnp.sum(part(recv5, span)[...].astype(F32), axis=0)
+        part(out_v, span)[...] = (part(hidden_v, span)[...] + total).astype(BF16)
+        write_out(c, span).start()
+
+    def pipeline(stages, pieces):
+        unit = features / 7
+        steps = [
+            ((span[0] + span[1]) / unit + LAGS[s], s, c, stage)
+            for s, stage in enumerate(stages)
+            for c, span in enumerate(pieces)
+        ]
         for _, _, c, stage in sorted(steps, key=lambda step: step[:3]):
-            stage(c)
-
-    pipeline([project, add_sibling, finish_hidden, forward, experts])
+            stage(c, pieces[c])
+
+    pipeline([project, add_sibling, finish_hidden, forward, experts], spans)
     activate()
-    pipeline([down, add_sibling_down, finish])
-
-    for c in range(chunks):
-        pltpu.make_async_copy(out_v.at[c], out_hbm.at[:, cols(c)], out_sem.at[c]).wait()
-        wait_bytes(send1.at[c], stage_send.at[0, c])
-        wait_bytes(send2.at[c], stage_send.at[1, c])
-        wait_bytes(peers(rows_own.at[c]), stage_send.at[2, c])
-        wait_bytes(rows_own.at[c], stage_send.at[3, c])
-        wait_bytes(send4.at[c], stage_send.at[4, c])
-        wait_bytes(send5.at[c], stage_send.at[5, c])
+    pipeline([down, add_sibling_down, finish], down_spans)
+
+    for c, span in enumerate(spans):
+        wait_bytes(part(send1, span), stage_send.at[0, c])
+        wait_bytes(part(send2, span), stage_send.at[1, c])
+        wait_bytes(peers(part(rows_own, span)), stage_send.at[2, c])
+        wait_bytes(part(rows_own, span), stage_send.at[3, c])
+    for c, span in enumerate(down_spans):
+        wait_bytes(part(send4, span), stage_send.at[4, c])
+        wait_bytes(part(send5, span), stage_send.at[5, c])
+        write_out(c, span).wait()
     wait_bytes(peers(meta_own), stage_send.at[2, chunks])
     wait_bytes(meta_own, stage_send.at[3, chunks])
 
@@ -270,20 +282,21 @@
     members, _, units = w_gate.shape
     chips = groups // 2 * tensors
     experts_all = groups * members
-    chunks = column_chunks(features)
-    width = features // chunks
-    dims = (chunks, width, chips, tensors, rows, members, experts_all)
+    spans = column_chunks(features, UNITS, True)
+    down_spans = column_chunks(features, UNITS, False)
+    chunks = max(len(spans), len(down_spans))
+    dims = (spans, down_spans, chips, tensors, rows, members, experts_all)
 
     def vmem(shape, dtype):
         return pltpu.VMEM(shape, dtype)
 
     exchange = [
-        vmem((chunks, chips, rows, width), F32),
-        vmem((chunks, chips, rows, width), BF16),
-        vmem((chunks, chips, rows, width), BF16),
-        vmem((chunks, rows, width), F32),
-        vmem((chunks, chips - 1, rows, width), BF16),
-        vmem((chunks, chips - 1, rows, width), BF16),
+        vmem((chips, rows, features), F32),
+        vmem((chips, rows, features), BF16),
+        vmem((chips, rows, features), BF16),
+        vmem((rows, features), F32),
+        vmem((chips - 1, rows, features), BF16),
+        vmem((chips - 1, rows, features), BF16),
     ]
     scratch = [
         vmem((tokens, heads), BF16),
@@ -293,23 +306,22 @@
         vmem((features,), F32),
         vmem(expert_ids.shape[::-1], expert_ids.dtype),
         vmem(gate_weights.shape[::-1], gate_weights.dtype),
-        vmem((chunks, heads, width), BF16),
-        vmem((chunks, members, width, units), BF16),
-        vmem((chunks, members, width, units), BF16),
-        vmem((chunks, members, units, width), BF16),
+        vmem((heads, features), BF16),
+        vmem((members, features, units), BF16),
+        vmem((members, features, units), BF16),
+        vmem((members, units, features), BF16),
         *exchange,
-        vmem((chunks, rows, width), F32),
-        vmem((rows, width), F32),
+        vmem((rows, features), F32),
         vmem((rows, META), F32),
-        vmem((chunks, chips, rows, width), BF16),
-        vmem((chunks, chips, rows, width), BF16),
+        vmem((chips, rows, features), BF16),
+        vmem((chips, rows, features), BF16),
         vmem((chips, rows, META), F32),
         vmem((chips, rows, META), F32),
         vmem((members, tokens, units), F32),
         vmem((members, tokens, units), F32),
         vmem((members, tokens, units), BF16),
         *exchange,
-        vmem((chunks, rows, width), BF16),
+        vmem((rows, features), BF16),
         pltpu.SemaphoreType.DMA((5,)),
         pltpu.SemaphoreType.DMA((chunks,)),
         pltpu.SemaphoreType.DMA((chunks,)),

time: 31.4 us -> 31.3 us (level)
  no operation moved by 1% of the time
where the time goes in v3:
time: 31.3 us; the launch traced here: 31.2 us
  Pallas kernels  29.7 us (95%)
  local copies, waits for them, and re-layouts  1.45 us (5%)
    pallas_call x1, Pallas kernels, on_device(): pl.pallas_call(functools.partial(kernel, dims), out_shape=jax.ShapeDtypeS...  29.7 us
    unnamed x1, local copies, waits for them, and re-layouts  1.45 us

profile of v3, /device:TPU:0, one launch (start us, length us, event | category | flops | bytes accessed | tf_op | source)
XLA Modules:
  0.0 31.2 jit_solution(14821943198835360510)
XLA Ops:
  0.0 29.7 %projected_experts.1 = bf16[8,3584]{1,0:T(8,128)(2,1)} custom-call(bf16[64,1024]{1,0:T(8,128)(2,1)} %attn_hbm.1, bf16[1024,3584]{1,0:T(8,128)(2,1)} %wo_hbm.1, bf16[8,3584]{1,0:T(8,128)(2,1)} %res_hbm.1, f32[3584]{0:T(1024)} %gain_hbm.1, s32[4,8]{1,0:T(4,128)} %bitcast.2, bf16[4,8]{1,0:T(4,128)(2,1)} %bitcast.3, bf16[2,3584,512]{2,1,0:T(8,128)(2,1)} %wg_hbm.1, ...), custom_call_target="tpu_custom_call" | custom-call | flops 1879048192 | bytes 29360128 | tf_op jit(solution)/shard_map/projected_experts/pallas_call | solution.py:335
  29.7 1.4 %copy.11 = bf16[8,3584]{1,0:T(8,128)(2,1)} copy(bf16[8,3584]{1,0:T(8,128)(2,1)} %projected_experts.1) | data formatting | bytes 114688

commit v4 on v3

--- a/solution.py
+++ b/solution.py
@@ -10,7 +10,7 @@
 MESH = pl.DeviceIdType.MESH
 F32 = jnp.float32
 BF16 = jnp.bfloat16
-UNITS = 4
+UNITS = 2
 META = 128
 LAGS = (0, 4, 10, 17, 21)
 
@@ -80,17 +80,25 @@
     wg_copies = fetches(wg_hbm, wg_v, wg_sem, spans, 1)
     wu_copies = fetches(wu_hbm, wu_v, wu_sem, spans, 1)
     wd_copies = fetches(wd_hbm, wd_v, wd_sem, down_spans, 2)
+    queue = list(wo_copies)
+    for gate_copy, up_copy in zip(wg_copies, wu_copies):
+        queue += [gate_copy, up_copy]
+    queue += wd_copies
+
+    def fetch_more(count):
+        for _ in range(min(count, len(queue))):
+            queue.pop(0).start()
+
+    def need(copy):
+        while any(copy is later for later in queue):
+            fetch_more(1)
+        copy.wait()
+
     smalls[0].start()
-    wo_copies[0].start()
+    fetch_more(1)
     for copy in smalls[1:]:
         copy.start()
-    for copy in wo_copies[1:]:
-        copy.start()
-    for c in range(chunks):
-        wg_copies[c].start()
-        wu_copies[c].start()
-    for copy in wd_copies:
-        copy.start()
+    fetch_more(2)
 
     def wait_bytes(ref, sem):
         pltpu.make_async_copy(ref, ref, sem).wait()
@@ -136,7 +144,7 @@
         send[...] = product[half:].reshape(chips, rows, width).astype(BF16)
 
     def project(c, span):
-        wo_copies[c].wait()
+        need(wo_copies[c])
         product = jnp.dot(attn_p[...], part(wo_v, span)[...], preferred_element_type=F32)
         split(product, part(keep1, span), part(send1, span))
         if c == 0:
@@ -196,8 +204,8 @@
             to_sibling(3, chunks, meta_own, meta_sib)
 
     def experts(c, span):
-        wg_copies[c].wait()
-        wu_copies[c].wait()
+        need(wg_copies[c])
+        need(wu_copies[c])
         wait_bytes(part(rows_sib, span), stage_recv.at[3, c])
         both = jnp.concatenate(
             [part(ref, span)[...].astype(F32).reshape(half, span[1]) for ref in (rows_own, rows_sib)], axis=0
@@ -222,7 +230,7 @@
             act_v[member] = (gate / (1.0 + jnp.exp(-gate)) * up * weight).astype(BF16)
 
     def down(c, span):
-        wd_copies[c].wait()
+        need(wd_copies[c])
         product = jnp.dot(act_v[0], part(wd_v, span)[0], preferred_element_type=F32)
         for member in range(1, members):
             product = product + jnp.dot(act_v[member], part(wd_v, span)[member], preferred_element_type=F32)
@@ -254,6 +262,7 @@
         ]
         for _, _, c, stage in sorted(steps, key=lambda step: step[:3]):
             stage(c, pieces[c])
+            fetch_more(1)
 
     pipeline([project, add_sibling, finish_hidden, forward, experts], spans)
     activate()

time: 31.3 us -> 27.3 us (0.87)
  Pallas kernels: 29.7 us -> 25.7 us
    pallas_call x1, Pallas kernels: 29.7 us -> 25.7 us  [on_device(): pl.pallas_call(functools.partial(kernel, dims), out_shape=jax.ShapeDtypeS...]
where the time goes in v4:
time: 27.3 us; the launch traced here: 27.1 us
  Pallas kernels  25.7 us (94%)
  local copies, waits for them, and re-layouts  1.45 us (5%)
    pallas_call x1, Pallas kernels, on_device(): pl.pallas_call(functools.partial(kernel, dims), out_shape=jax.ShapeDtypeS...  25.7 us
    unnamed x1, local copies, waits for them, and re-layouts  1.45 us

profile of v4, /device:TPU:0, one launch (start us, length us, event | category | flops | bytes accessed | tf_op | source)
XLA Modules:
  0.0 27.1 jit_solution(3146273110928958875)
XLA Ops:
  0.0 25.7 %projected_experts.1 = bf16[8,3584]{1,0:T(8,128)(2,1)} custom-call(bf16[64,1024]{1,0:T(8,128)(2,1)} %attn_hbm.1, bf16[1024,3584]{1,0:T(8,128)(2,1)} %wo_hbm.1, bf16[8,3584]{1,0:T(8,128)(2,1)} %res_hbm.1, f32[3584]{0:T(1024)} %gain_hbm.1, s32[4,8]{1,0:T(4,128)} %bitcast.2, bf16[4,8]{1,0:T(4,128)(2,1)} %bitcast.3, bf16[2,3584,512]{2,1,0:T(8,128)(2,1)} %wg_hbm.1, ...), custom_call_target="tpu_custom_call" | custom-call | flops 1879048192 | bytes 29360128 | tf_op jit(solution)/shard_map/projected_experts/pallas_call | solution.py:344
  25.7 1.4 %copy.11 = bf16[8,3584]{1,0:T(8,128)(2,1)} copy(bf16[8,3584]{1,0:T(8,128)(2,1)} %projected_experts.1) | data formatting | bytes 114688

commit v5 on v4

--- a/solution.py
+++ b/solution.py
@@ -253,6 +253,13 @@
         part(out_v, span)[...] = (part(hidden_v, span)[...] + total).astype(BF16)
         write_out(c, span).start()
 
+    def fetches_after(stage, c):
+        if stage is project:
+            return 1 if c < chunks - 3 else 0
+        if stage is add_sibling:
+            return 2 if c == chunks - 1 else 0
+        return 1
+
     def pipeline(stages, pieces):
         unit = features / 7
         steps = [
@@ -262,7 +269,7 @@
         ]
         for _, _, c, stage in sorted(steps, key=lambda step: step[:3]):
             stage(c, pieces[c])
-            fetch_more(1)
+            fetch_more(fetches_after(stage, c))
 
     pipeline([project, add_sibling, finish_hidden, forward, experts], spans)
     activate()

time: 27.3 us -> 27.3 us (level)
  no operation moved by 1% of the time
where the time goes in v5:
time: 27.3 us; the launch traced here: 27.1 us
  Pallas kernels  25.7 us (94%)
  local copies, waits for them, and re-layouts  1.45 us (5%)
    pallas_call x1, Pallas kernels, on_device(): pl.pallas_call(functools.partial(kernel, dims), out_shape=jax.ShapeDtypeS...  25.7 us
    unnamed x1, local copies, waits for them, and re-layouts  1.45 us

profile of v5, /device:TPU:0, one launch (start us, length us, event | category | flops | bytes accessed | tf_op | source)
XLA Modules:
  0.0 27.1 jit_solution(7115681646341650222)
XLA Ops:
  0.0 25.7 %projected_experts.1 = bf16[8,3584]{1,0:T(8,128)(2,1)} custom-call(bf16[64,1024]{1,0:T(8,128)(2,1)} %attn_hbm.1, bf16[1024,3584]{1,0:T(8,128)(2,1)} %wo_hbm.1, bf16[8,3584]{1,0:T(8,128)(2,1)} %res_hbm.1, f32[3584]{0:T(1024)} %gain_hbm.1, s32[4,8]{1,0:T(4,128)} %bitcast.2, bf16[4,8]{1,0:T(4,128)(2,1)} %bitcast.3, bf16[2,3584,512]{2,1,0:T(8,128)(2,1)} %wg_hbm.1, ...), custom_call_target="tpu_custom_call" | custom-call | flops 1879048192 | bytes 29360128 | tf_op jit(solution)/shard_map/projected_experts/pallas_call | solution.py:351
  25.7 1.4 %copy.11 = bf16[8,3584]{1,0:T(8,128)(2,1)} copy(bf16[8,3584]{1,0:T(8,128)(2,1)} %projected_experts.1) | data formatting | bytes 114688

commit v6 on v5

--- a/solution.py
+++ b/solution.py
@@ -12,7 +12,7 @@
 BF16 = jnp.bfloat16
 UNITS = 2
 META = 128
-LAGS = (0, 4, 10, 17, 21)
+LAGS = (0, 3, 9, 15, 18)
 
 
 def column_chunks(features, units, first_short):

time: 27.3 us -> 26.7 us (0.978)
  Pallas kernels: 25.7 us -> 25.1 us
    pallas_call x1, Pallas kernels: 25.7 us -> 25.1 us  [on_device(): pl.pallas_call(functools.partial(kernel, dims), out_shape=jax.ShapeDtypeS...]
where the time goes in v6:
time: 26.7 us; the launch traced here: 26.5 us
  Pallas kernels  25.1 us (94%)
  local copies, waits for them, and re-layouts  1.45 us (5%)
    pallas_call x1, Pallas kernels, on_device(): pl.pallas_call(functools.partial(kernel, dims), out_shape=jax.ShapeDtypeS...  25.1 us
    unnamed x1, local copies, waits for them, and re-layouts  1.45 us

profile of v6, /device:TPU:0, one launch (start us, length us, event | category | flops | bytes accessed | tf_op | source)
XLA Modules:
  0.0 26.5 jit_solution(1200329121612846313)
XLA Ops:
  0.0 25.1 %projected_experts.1 = bf16[8,3584]{1,0:T(8,128)(2,1)} custom-call(bf16[64,1024]{1,0:T(8,128)(2,1)} %attn_hbm.1, bf16[1024,3584]{1,0:T(8,128)(2,1)} %wo_hbm.1, bf16[8,3584]{1,0:T(8,128)(2,1)} %res_hbm.1, f32[3584]{0:T(1024)} %gain_hbm.1, s32[4,8]{1,0:T(4,128)} %bitcast.2, bf16[4,8]{1,0:T(4,128)(2,1)} %bitcast.3, bf16[2,3584,512]{2,1,0:T(8,128)(2,1)} %wg_hbm.1, ...), custom_call_target="tpu_custom_call" | custom-call | flops 1879048192 | bytes 29360128 | tf_op jit(solution)/shard_map/projected_experts/pallas_call | solution.py:351
  25.1 1.4 %copy.11 = bf16[8,3584]{1,0:T(8,128)(2,1)} copy(bf16[8,3584]{1,0:T(8,128)(2,1)} %projected_experts.1) | data formatting | bytes 114688

commit v7 on v6

--- a/solution.py
+++ b/solution.py
@@ -12,7 +12,7 @@
 BF16 = jnp.bfloat16
 UNITS = 2
 META = 128
-LAGS = (0, 3, 9, 15, 18)
+LAGS = (0, 2, 8, 14, 16)
 
 
 def column_chunks(features, units, first_short):
@@ -28,13 +28,13 @@
 def kernel(
     dims,
     attn_hbm, wo_hbm, res_hbm, gain_hbm, ids_hbm, gw_hbm, wg_hbm, wu_hbm, wd_hbm,
-    out_hbm,
+    base_hbm, landed_hbm,
     attn_v, attn_blocks, attn_p, res_v, gain_v, ids_v, gw_v,
     wo_v, wg_v, wu_v, wd_v,
     keep1, send1, recv1, own2, send2, recv2, hidden_v, table_v,
     rows_own, rows_sib, meta_own, meta_sib,
     acc_gate, acc_up, act_v,
-    keep4, send4, recv4, own5, send5, recv5, out_v,
+    keep4, send4, recv4, own5, send5,
     small_sem, wo_sem, wg_sem, wu_sem, wd_sem, out_sem,
     stage_send, stage_recv,
 ):
@@ -240,18 +240,13 @@
     def add_sibling_down(c, span):
         wait_bytes(part(recv4, span), stage_recv.at[4, c])
         total = part(keep4, span)[...] + part(recv4, span)[...].astype(F32)
-        part(own5, span)[...] = total[0]
+        part(own5, span)[...] = part(hidden_v, span)[...] + total[0]
         part(send5, span)[...] = total[1:].astype(BF16)
-        to_owners(5, c, part(send5, span), part(recv5, span))
-
-    def write_out(c, span):
-        return pltpu.make_async_copy(part(out_v, span), part(out_hbm, span), out_sem.at[c])
-
-    def finish(c, span):
-        wait_bytes(part(recv5, span), stage_recv.at[5, c])
-        total = part(own5, span)[...] + jnp.sum(part(recv5, span)[...].astype(F32), axis=0)
-        part(out_v, span)[...] = (part(hidden_v, span)[...] + total).astype(BF16)
-        write_out(c, span).start()
+        write_base(c, span).start()
+        to_owners(5, c, part(send5, span), part(landed_hbm, span))
+
+    def write_base(c, span):
+        return pltpu.make_async_copy(part(own5, span), part(base_hbm, span), out_sem.at[c])
 
     def fetches_after(stage, c):
         if stage is project:
@@ -273,7 +268,7 @@
 
     pipeline([project, add_sibling, finish_hidden, forward, experts], spans)
     activate()
-    pipeline([down, add_sibling_down, finish], down_spans)
+    pipeline([down, add_sibling_down], down_spans)
 
     for c, span in enumerate(spans):
         wait_bytes(part(send1, span), stage_send.at[0, c])
@@ -283,7 +278,8 @@
     for c, span in enumerate(down_spans):
         wait_bytes(part(send4, span), stage_send.at[4, c])
         wait_bytes(part(send5, span), stage_send.at[5, c])
-        write_out(c, span).wait()
+        write_base(c, span).wait()
+        wait_bytes(part(landed_hbm, span), stage_recv.at[5, c])
     wait_bytes(peers(meta_own), stage_send.at[2, chunks])
     wait_bytes(meta_own, stage_send.at[3, chunks])
 
@@ -336,8 +332,7 @@
         vmem((members, tokens, units), F32),
         vmem((members, tokens, units), F32),
         vmem((members, tokens, units), BF16),
-        *exchange,
-        vmem((rows, features), BF16),
+        *exchange[:-1],
         pltpu.SemaphoreType.DMA((5,)),
         pltpu.SemaphoreType.DMA((chunks,)),
         pltpu.SemaphoreType.DMA((chunks,)),
@@ -348,11 +343,14 @@
         pltpu.SemaphoreType.DMA((6, chunks + 1)),
     ]
     weights = out_proj.size + w_gate.size + w_up.size + w_down.size
-    return pl.pallas_call(
+    base, landed = pl.pallas_call(
         functools.partial(kernel, dims),
-        out_shape=jax.ShapeDtypeStruct((rows, features), BF16),
+        out_shape=(
+            jax.ShapeDtypeStruct((rows, features), F32),
+            jax.ShapeDtypeStruct((chips - 1, rows, features), BF16),
+        ),
         in_specs=[pl.BlockSpec(memory_space=pl.ANY)] * 9,
-        out_specs=pl.BlockSpec(memory_space=pl.ANY),
+        out_specs=[pl.BlockSpec(memory_space=pl.ANY)] * 2,
         scratch_shapes=scratch,
         cost_estimate=pl.CostEstimate(
             flops=2 * tokens * weights, bytes_accessed=2 * weights, transcendentals=0
@@ -365,6 +363,10 @@
         attn_heads, out_proj, residual_in, norm_gain,
         expert_ids.T, gate_weights.T, w_gate, w_up, w_down,
     )
+    total = base
+    for i in range(chips - 1):
+        total = total + landed[i].astype(F32)
+    return total.astype(BF16)
 
 
 def solution(mesh):

time: 26.7 us -> 26.2 us (0.981)
  other arithmetic: 0 us -> 1.59 us
  local copies, waits for them, and re-layouts: 1.45 us -> 0 us
  Pallas kernels: 25.1 us -> 24.4 us
    convert_element_type x0 -> x1, other arithmetic: none -> 1.59 us  [on_device(): return total.astype(BF16)]
    unnamed x1 -> x0, local copies, waits for them, and re-layouts: 1.45 us -> none
    pallas_call x1, Pallas kernels: 25.1 us -> 24.4 us  [on_device(): pl.pallas_call(functools.partial(kernel, dims), out_shape=(jax.ShapeDtype...]
where the time goes in v7:
time: 26.2 us; the launch traced here: 26 us
  Pallas kernels  24.4 us (93%)
  other arithmetic  1.59 us (6%)
    pallas_call x1, Pallas kernels, on_device(): pl.pallas_call(functools.partial(kernel, dims), out_shape=(jax.ShapeDtype...  24.4 us
    convert_element_type x1, other arithmetic, on_device(): return total.astype(BF16)  1.59 us

profile of v7, /device:TPU:0, one launch (start us, length us, event | category | flops | bytes accessed | tf_op | source)
XLA Modules:
  0.0 26.0 jit_solution(13141485309954152074)
XLA Ops:
  0.0 24.4 %projected_experts.1 = (f32[8,3584]{1,0:T(8,128)}, bf16[3,8,3584]{2,1,0:T(8,128)(2,1)}) custom-call(bf16[64,1024]{1,0:T(8,128)(2,1)} %attn_hbm.1, bf16[1024,3584]{1,0:T(8,128)(2,1)} %wo_hbm.1, bf16[8,3584]{1,0:T(8,128)(2,1)} %res_hbm.1, f32[3584]{0:T(1024)} %gain_hbm.1, s32[4,8]{1,0:T(4,128)} %bitcast.11, bf16[4,8]{1,0:T(4,128)(2,1)} %bitcast.12, ...), custom_call_target="tpu_custom_call" | custom-call | flops 1879048192 | bytes 29360128 | tf_op jit(solution)/shard_map/projected_experts/pallas_call | solution.py:346
  24.4 1.6 %fusion = bf16[8,3584]{1,0:T(8,128)(2,1)} fusion(f32[8,3584]{1,0:T(8,128)} %get-tuple-element.7, bf16[3,8,3584]{2,1,0:T(8,128)(2,1)} %get-tuple-element.8), kind=kLoop, calls=%fused_computation.1 | loop fusion | flops 200704 | bytes 344064 | tf_op jit(solution)/shard_map/convert_element_type | solution.py:369
